TPU v7x, 32 devices: a whole 2x2x4 slice. The times are simulated.
32 devices in a mesh: grp: 2 (over y), seq: 4 (over x, core), kvh: 4 (over z).
Axes of the slice: x: 2, y: 2, z: 4, core: 2. Of those that a mesh axis runs over, the one named last changes fastest.
Arguments:
- queries: bfloat16 [2048, 8192], P(('grp', 'seq'), 'kvh'), parts along dimension 0, may hold values from -150 to 150
- keys_values: bfloat16 [2, 2048, 1024], P(None, ('grp', 'seq'), 'kvh'), parts along dimension 1, may hold values from -5 to 5
- band_widths: int32 [128], P(('grp', 'kvh')), parts along dimension 0, may hold values from 128 to 2048, as said below
- summary_blocks: int32 [8], P('grp'), parts along dimension 0, may hold values from 0 to 7, as said below
Outputs:
- attended: bfloat16 [2048, 8192], P(('grp', 'seq'), 'kvh'), parts along dimension 0
There are 2 independent parts, one for each index of `grp`. A program takes and returns all parts, laid end to end along the dimension named above; each array names one. Nothing has to cross between parts.
Inputs may be any that keep to these rules, and one draw needn't show every extreme that they name: `band_widths`: some head has a band of exactly 2048 keys in every draw. `summary_blocks`: entry j names a block within positions j * 256 to (j + 1) * 256 - 1.
All inputs are finite; a program needn't handle non-finite values.
Results may differ from a plain program's by a relative error of at most 0.0029.
Values may be sent and summed in bfloat16 or wider, within the bound.
A program may use at most 64 MiB of HBM per device.

v0:
```python
import functools
import math

import jax
import jax.numpy as jnp
from jax import lax
from jax.experimental import pallas as pl
from jax.experimental.pallas import tpu as pltpu
from jax.sharding import PartitionSpec as P

HD = 128
BAND = 2048
SB = 128
ONES = 16
STAT = 8
ALWAYS = 1 << 28
HEAD_UNROLL = 4


very_low = -1e30


def from_behind(block, axis, distance):
    devices = range(lax.axis_size(axis))
    route = [(i - distance, i) for i in devices if i - distance in devices]
    return lax.ppermute(block, axis, route)


def absorb(running, shard_rows, key_pos, summary, grouped, limits, query_pos):
    count = shard_rows.shape[1]
    width = math.gcd(count, 512)
    pieces = count // width
    heads_kv = grouped.shape[1]
    head_dim = grouped.shape[3]
    blocked = jnp.moveaxis(shard_rows.reshape(2, pieces, width, heads_kv, head_dim), 1, 0)
    positions = key_pos.reshape(pieces, width)

    def absorb_block(carried, item):
        block_rows, block_pos = item
        best, total, accum = carried
        scores = jnp.einsum(
            "cgrd,kgd->grck", grouped, block_rows[0], preferred_element_type=jnp.float32
        ) * head_dim ** (-0.5)
        key_line = block_pos[None, None, None, :]
        if summary:
            visible = key_line <= limits[:, :, :, None]
        else:
            visible = (
                (key_line > limits[:, :, :, None])
                & (key_line <= query_pos[None, None, :, None])
                & (key_line >= 0)
            )
        new_best = jnp.maximum(best, jnp.max(jnp.where(visible, scores, very_low), axis=-1))
        weights = jnp.where(visible, jnp.exp(scores - new_best[:, :, :, None]), 0.0)
        fade = jnp.exp(best - new_best)
        total = total * fade + jnp.sum(weights, axis=-1)
        accum = accum * fade[:, :, :, None] + jnp.einsum(
            "grck,kgd->grcd",
            weights.astype(jnp.bfloat16),
            block_rows[1],
            preferred_element_type=jnp.float32,
        )
        return ((new_best, total, accum), None)

    running, unused = lax.scan(absorb_block, running, (blocked, positions))
    return running


def body(queries, keys_values, band_widths, summary_blocks):
    rows = queries.shape[0]
    heads_kv = keys_values.shape[2] // HD
    heads_dev = band_widths.shape[0]
    ratio = heads_dev // heads_kv
    seq_index = lax.axis_index("seq")
    query_pos = seq_index * rows + jnp.arange(rows, dtype=jnp.int32)
    grouped = queries.reshape(rows, heads_kv, ratio, HD)
    limits = query_pos[None, None, :] - band_widths.reshape(heads_kv, ratio)[:, :, None]
    running = (
        jnp.full((heads_kv, ratio, rows), very_low, jnp.float32),
        jnp.zeros((heads_kv, ratio, rows), jnp.float32),
        jnp.zeros((heads_kv, ratio, rows, HD), jnp.float32),
    )
    reach = (BAND - 1) // rows + 1
    local_iota = jnp.arange(rows, dtype=jnp.int32)
    running = absorb(running, keys_values, query_pos, False, grouped, limits, query_pos)
    for distance in range(1, reach + 1):
        earlier = from_behind(keys_values, "seq", distance)
        running = absorb(
            running,
            earlier,
            (seq_index - distance) * rows + local_iota,
            False,
            grouped,
            limits,
            query_pos,
        )
    own_block = lax.dynamic_index_in_dim(summary_blocks, seq_index, 0, keepdims=False)
    local_block = own_block - seq_index * (rows // SB)
    summary_rows = lax.dynamic_slice_in_dim(keys_values, local_block * SB, SB, 1)
    summary_pos = (summary_blocks[:, None] * SB + jnp.arange(SB, dtype=jnp.int32)[None, :]).reshape(
        -1
    )
    gathered = lax.all_gather(summary_rows, "seq", axis=1, tiled=True)
    running = absorb(running, gathered, summary_pos, True, grouped, limits, query_pos)
    best, total, accum = running
    result = accum / total[:, :, :, None]
    return jnp.transpose(result, (2, 0, 1, 3)).reshape(rows, heads_dev * HD).astype(jnp.bfloat16)


def attend_kernel(
    rows, heads_kv, ratio, q_hbm, kv_hbm, widths, blocks, out_hbm,
    q_buf, kv_buf, vt_buf, acc_buf, best_buf, key_buf, out_buf,
    q_sem, own_sem, out_sem, near_send, far_send, pass_send, recv_sem,
):
    me = lax.axis_index("seq")
    core = lax.rem(me, 2)
    partner = me + 1 - 2 * core
    seq_size = lax.axis_size("seq")
    heads = heads_kv * ratio
    scale = math.log2(math.e) * HD ** (-0.5)

    def remote(src, slot, g, send_sem, target):
        return pltpu.make_async_remote_copy(
            src_ref=src,
            dst_ref=kv_buf.at[slot, g],
            send_sem=send_sem,
            recv_sem=recv_sem.at[slot, g],
            device_id={"seq": target},
            device_id_type=pl.DeviceIdType.MESH,
        )

    def own_rows(g):
        return kv_hbm.at[:, :, g * HD : (g + 1) * HD]

    def own_copy(g):
        return pltpu.make_async_copy(own_rows(g), kv_buf.at[me, g], own_sem.at[g])

    def q_copy(h):
        return pltpu.make_async_copy(
            q_hbm.at[:, h * HD : (h + 1) * HD], q_buf.at[h], q_sem.at[h]
        )

    barrier = pltpu.get_barrier_semaphore()
    for step in range(1, seq_size):
        pl.semaphore_signal(
            barrier,
            inc=1,
            device_id={"seq": lax.rem(me + step, seq_size)},
            device_id_type=pl.DeviceIdType.MESH,
        )
    for g in range(heads_kv):
        own_copy(g).start()
    for h in range(heads):
        q_copy(h).start()
    pl.semaphore_wait(barrier, seq_size - 1)

    for g in range(heads_kv):

        @pl.when(me < 2)
        def _():
            remote(own_rows(g), me, g, far_send.at[g], me + 2).start()

        @pl.when(core == 0)
        def _():
            remote(own_rows(g), me, g, near_send.at[g], me + 1).start()

    for slot in range(seq_size):
        pos = slot * rows + lax.broadcasted_iota(jnp.int32, (rows, HD), 0)
        first = blocks[slot] * SB
        in_summary = (pos >= first) & (pos < first + SB)
        key_buf[slot] = jnp.where(in_summary, ALWAYS, pos)
    for g in range(heads_kv):
        vt_buf[g, HD:, :] = jnp.ones((ONES, rows), jnp.bfloat16)

    row_pos = me * rows + lax.broadcasted_iota(jnp.int32, (1, rows), 1)

    def heads_of(slot, g, is_own):
        vt_buf[g, :HD, :] = kv_buf[slot, g, 1].astype(jnp.float32).T.astype(jnp.bfloat16)

        def one_head(r, unused):
            h = g * ratio + r
            scores = lax.dot_general(
                kv_buf[slot, g, 0],
                q_buf[h],
                (((1,), (1,)), ((), ())),
                preferred_element_type=jnp.float32,
            )
            limit = row_pos - widths[h]
            lanes = key_buf[slot]
            keys = jnp.concatenate([lanes] * (rows // HD), axis=1)
            visible = keys > limit
            if is_own:
                visible = visible & (
                    lax.broadcasted_iota(jnp.int32, (rows, rows), 0)
                    <= lax.broadcasted_iota(jnp.int32, (rows, rows), 1)
                )
            scores = jnp.where(visible, scores, -1e30)
            top = jnp.max(scores, axis=0, keepdims=True)
            if not is_own:
                old = best_buf[h]
                top = jnp.maximum(old, top)
            weights = jnp.exp2((scores - top) * scale).astype(jnp.bfloat16)
            part = lax.dot_general(
                vt_buf[g],
                weights,
                (((1,), (0,)), ((), ())),
                preferred_element_type=jnp.float32,
            )[: HD + STAT]
            if not is_own:
                part = part + acc_buf[h] * jnp.exp2((old - top) * scale)
            acc_buf[h] = part
            best_buf[h] = top
            return unused

        lax.fori_loop(0, ratio, one_head, 0, unroll=HEAD_UNROLL)

    for g in range(heads_kv):
        own_copy(g).wait()
    for h in range(heads):
        q_copy(h).wait()

    def own_step(g, unused):
        heads_of(me, g, True)
        return unused

    lax.fori_loop(0, heads_kv, own_step, 0)

    near = heads_kv * core

    def other_step(item, unused):
        far = item - near
        is_near = item < near
        far_slot = jnp.where(lax.rem(far, 2) == 0, core, 1 - core)
        slot = jnp.where(is_near, me - 1, far_slot)
        g = jnp.where(is_near, item, far // 2)
        remote(kv_buf.at[slot, g], slot, g, pass_send.at[g], partner).wait_recv()

        @pl.when((me >= 2) & (slot == core))
        def _():
            remote(kv_buf.at[slot, g], slot, g, pass_send.at[g], partner).start()

        heads_of(slot, g, False)
        return unused

    lax.fori_loop(0, heads_kv * me, other_step, 0)

    def out_copy(h):
        return pltpu.make_async_copy(
            out_buf.at[h],
            out_hbm.at[:, pl.ds(pl.multiple_of(h * HD, HD), HD)],
            out_sem.at[h],
        )

    def finish(h, unused):
        total = acc_buf[h, HD : HD + 1, :]
        result = acc_buf[h, :HD, :] * (1.0 / total)
        out_buf[h] = result.T.astype(jnp.bfloat16)
        out_copy(h).start()
        return unused

    lax.fori_loop(0, heads, finish, 0, unroll=4)

    for g in range(heads_kv):

        @pl.when(me < 2)
        def _():
            remote(own_rows(g), me, g, far_send.at[g], me + 2).wait_send()

        @pl.when(core == 0)
        def _():
            remote(own_rows(g), me, g, near_send.at[g], me + 1).wait_send()

        @pl.when(me >= 2)
        def _():
            remote(kv_buf.at[core, g], core, g, pass_send.at[g], partner).wait_send()

    for h in range(heads):
        out_copy(h).wait()


def fused_body(queries, keys_values, band_widths, summary_blocks):
    rows = queries.shape[0]
    heads_kv = keys_values.shape[2] // HD
    heads = band_widths.shape[0]
    seq_size = lax.axis_size("seq")
    anywhere = pl.BlockSpec(memory_space=pl.ANY)
    scalars = pl.BlockSpec(memory_space=pltpu.SMEM)
    dma = pltpu.SemaphoreType.DMA
    return pl.pallas_call(
        functools.partial(attend_kernel, rows, heads_kv, heads // heads_kv),
        out_shape=jax.ShapeDtypeStruct(queries.shape, jnp.bfloat16),
        in_specs=[anywhere, anywhere, scalars, scalars],
        out_specs=anywhere,
        scratch_shapes=[
            pltpu.VMEM((heads, rows, HD), jnp.bfloat16),
            pltpu.VMEM((seq_size, heads_kv, 2, rows, HD), jnp.bfloat16),
            pltpu.VMEM((heads_kv, HD + ONES, rows), jnp.bfloat16),
            pltpu.VMEM((heads, HD + STAT, rows), jnp.float32),
            pltpu.VMEM((heads, 1, rows), jnp.float32),
            pltpu.VMEM((seq_size, rows, HD), jnp.int32),
            pltpu.VMEM((heads, rows, HD), jnp.bfloat16),
            dma((heads,)),
            dma((heads_kv,)),
            dma((heads,)),
            dma((heads_kv,)),
            dma((heads_kv,)),
            dma((heads_kv,)),
            dma((seq_size, heads_kv)),
        ],
        compiler_params=pltpu.CompilerParams(
            collective_id=0,
            has_side_effects=True,
            vmem_limit_bytes=32 * 1024 * 1024,
        ),
        cost_estimate=pl.CostEstimate(
            flops=4 * heads * rows * rows * seq_size * HD,
            bytes_accessed=4 * queries.size,
            transcendentals=heads * rows * rows * seq_size,
        ),
    )(queries, keys_values, band_widths, summary_blocks)


def dispatch(queries, keys_values, band_widths, summary_blocks):
    rows = queries.shape[0]
    seq_size = lax.axis_size("seq")
    two_chips = seq_size == 4 and summary_blocks.shape[0] == seq_size
    if two_chips and seq_size * rows <= BAND and rows % (2 * SB) == 0:
        return fused_body(queries, keys_values, band_widths, summary_blocks)
    return body(queries, keys_values, band_widths, summary_blocks)


def solution(mesh):
    return jax.shard_map(
        dispatch,
        mesh=mesh,
        in_specs=(
            P(("grp", "seq"), "kvh"),
            P(None, ("grp", "seq"), "kvh"),
            P(("grp", "kvh")),
            P("grp"),
        ),
        out_specs=P(("grp", "seq"), "kvh"),
        check_vma=False,
    )
```

profile of v0, /device:TPU:31, one launch (start us, length us, event | category | flops | bytes accessed | tf_op | source)
XLA Modules:
  0.0 30.0 jit_solution(11982328965836615540)
XLA Ops:
  0.0 0.0 copy-start
  0.0 1.2 %copy-done = bf16[256,2048]{1,0:T(8,128)(2,1)S(1)} copy-done((bf16[256,2048]{1,0:T(8,128)(2,1)S(1)}, bf16[256,2048]{1,0:T(8,128)(2,1)}, u32[]{:S(2)}) %copy-start) | copy-done | bytes 1048600
  1.2 0.0 copy-start.1
  1.2 0.9 %copy-done.1 = bf16[2,256,256]{2,1,0:T(8,128)(2,1)S(1)} copy-done((bf16[2,256,256]{2,1,0:T(8,128)(2,1)S(1)}, bf16[2,256,256]{2,1,0:T(8,128)(2,1)}, u32[]{:S(2)}) %copy-start.1) | copy-done | bytes 262168
  2.2 0.0 copy-start.2
  2.2 0.7 %copy-done.2 = s32[16]{0:T(128)S(1)} copy-done((s32[16]{0:T(128)S(1)}, s32[16]{0:T(128)}, u32[]{:S(2)}) %copy-start.2) | copy-done | bytes 88
  2.8 0.0 copy-start.3
  2.8 0.7 %copy-done.3 = s32[4]{0:T(128)S(1)} copy-done((s32[4]{0:T(128)S(1)}, s32[4]{0:T(128)}, u32[]{:S(2)}) %copy-start.3) | copy-done | bytes 40
  3.5 25.5 %shard_map.46 = bf16[256,2048]{1,0:T(8,128)(2,1)S(1)} custom-call(bf16[256,2048]{1,0:T(8,128)(2,1)S(1)} %copy-done, bf16[2,256,256]{2,1,0:T(8,128)(2,1)S(1)} %copy-done.1, s32[16]{0:T(128)S(1)} %copy-done.2, s32[4]{0:T(128)S(1)} %copy-done.3), custom_call_target="tpu_custom_call" | custom-call | flops 2147483648 | bytes 2097152 | tf_op jit(solution)/shard_map/pallas_call | solution.py:289
  29.0 1.0 %copy.6 = bf16[256,2048]{1,0:T(8,128)(2,1)} copy(bf16[256,2048]{1,0:T(8,128)(2,1)S(1)} %shard_map.46) | data formatting | bytes 2097152
Async XLA Ops:
  0.0 1.2 %copy-start = (bf16[256,2048]{1,0:T(8,128)(2,1)S(1)}, bf16[256,2048]{1,0:T(8,128)(2,1)}, u32[]{:S(2)}) copy-start(bf16[256,2048]{1,0:T(8,128)(2,1)} %q_hbm.1) | copy-start | bytes 3145732
  1.2 0.9 %copy-start.1 = (bf16[2,256,256]{2,1,0:T(8,128)(2,1)S(1)}, bf16[2,256,256]{2,1,0:T(8,128)(2,1)}, u32[]{:S(2)}) copy-start(bf16[2,256,256]{2,1,0:T(8,128)(2,1)} %kv_hbm.1) | copy-start | bytes 786436
  2.2 0.7 %copy-start.2 = (s32[16]{0:T(128)S(1)}, s32[16]{0:T(128)}, u32[]{:S(2)}) copy-start(s32[16]{0:T(128)} %widths.1) | copy-start | bytes 196
  2.8 0.7 %copy-start.3 = (s32[4]{0:T(128)S(1)}, s32[4]{0:T(128)}, u32[]{:S(2)}) copy-start(s32[4]{0:T(128)} %blocks.1) | copy-start | bytes 52
where the time goes:
time: 30.2 us; the launch traced here: 30 us
  Pallas kernels  25.5 us (84%)
  local copies, waits for them, and re-layouts  4.46 us (15%)
    pallas_call x1, Pallas kernels, fused_body(): pl.pallas_call(functools.partial(attend_kernel, rows, heads_kv, heads //...  25.5 us
    unnamed x9, local copies, waits for them, and re-layouts  4.46 us

commit v1 on v0

--- a/solution.py
+++ b/solution.py
@@ -14,7 +14,6 @@
 ONES = 16
 STAT = 8
 ALWAYS = 1 << 28
-HEAD_UNROLL = 4
 
 
 very_low = -1e30
@@ -109,7 +108,7 @@
 
 def attend_kernel(
     rows, heads_kv, ratio, q_hbm, kv_hbm, widths, blocks, out_hbm,
-    q_buf, kv_buf, vt_buf, acc_buf, best_buf, key_buf, out_buf,
+    q_buf, kv_buf, vt_buf, acc_buf, best_buf, key_buf, own_keys, out_buf,
     q_sem, own_sem, out_sem, near_send, far_send, pass_send, recv_sem,
 ):
     me = lax.axis_index("seq")
@@ -137,7 +136,9 @@
 
     def q_copy(h):
         return pltpu.make_async_copy(
-            q_hbm.at[:, h * HD : (h + 1) * HD], q_buf.at[h], q_sem.at[h]
+            q_hbm.at[:, h * HD : (h + 1) * HD],
+            q_buf.at[h // ratio, h % ratio],
+            q_sem.at[h],
         )
 
     barrier = pltpu.get_barrier_semaphore()
@@ -169,6 +170,10 @@
         first = blocks[slot] * SB
         in_summary = (pos >= first) & (pos < first + SB)
         key_buf[slot] = jnp.where(in_summary, ALWAYS, pos)
+    own_cols = lax.broadcasted_iota(jnp.int32, (rows, rows), 1)
+    own_down = lax.broadcasted_iota(jnp.int32, (rows, rows), 0)
+    own_line = jnp.concatenate([key_buf[me]] * (rows // HD), axis=1)
+    own_keys[...] = jnp.where(own_down <= own_cols, own_line, -ALWAYS)
     for g in range(heads_kv):
         vt_buf[g, HD:, :] = jnp.ones((ONES, rows), jnp.bfloat16)
 
@@ -177,42 +182,50 @@
     def heads_of(slot, g, is_own):
         vt_buf[g, :HD, :] = kv_buf[slot, g, 1].astype(jnp.float32).T.astype(jnp.bfloat16)
 
-        def one_head(r, unused):
-            h = g * ratio + r
-            scores = lax.dot_general(
+        def score(r):
+            return lax.dot_general(
                 kv_buf[slot, g, 0],
-                q_buf[h],
+                q_buf[g, r],
                 (((1,), (1,)), ((), ())),
                 preferred_element_type=jnp.float32,
             )
-            limit = row_pos - widths[h]
-            lanes = key_buf[slot]
-            keys = jnp.concatenate([lanes] * (rows // HD), axis=1)
-            visible = keys > limit
+
+        def soften(r, scores):
+            limit = row_pos - widths[g * ratio + r]
             if is_own:
-                visible = visible & (
-                    lax.broadcasted_iota(jnp.int32, (rows, rows), 0)
-                    <= lax.broadcasted_iota(jnp.int32, (rows, rows), 1)
-                )
-            scores = jnp.where(visible, scores, -1e30)
+                keys = own_keys[...]
+            else:
+                keys = jnp.concatenate([key_buf[slot]] * (rows // HD), axis=1)
+            scores = jnp.where(keys > limit, scores, -1e30)
             top = jnp.max(scores, axis=0, keepdims=True)
+            fade = None
             if not is_own:
-                old = best_buf[h]
+                old = best_buf[g, r]
                 top = jnp.maximum(old, top)
-            weights = jnp.exp2((scores - top) * scale).astype(jnp.bfloat16)
+                fade = jnp.exp2((old - top) * scale)
+            best_buf[g, r] = top
+            return jnp.exp2((scores - top) * scale).astype(jnp.bfloat16), fade
+
+        def mix(r, weights, fade):
             part = lax.dot_general(
                 vt_buf[g],
                 weights,
                 (((1,), (0,)), ((), ())),
                 preferred_element_type=jnp.float32,
             )[: HD + STAT]
-            if not is_own:
-                part = part + acc_buf[h] * jnp.exp2((old - top) * scale)
-            acc_buf[h] = part
-            best_buf[h] = top
-            return unused
-
-        lax.fori_loop(0, ratio, one_head, 0, unroll=HEAD_UNROLL)
+            if fade is not None:
+                part = part + acc_buf[g, r] * fade
+            acc_buf[g, r] = part
+
+        scores = score(0)
+        waiting = None
+        for r in range(ratio):
+            following = score(r + 1) if r + 1 < ratio else None
+            if waiting is not None:
+                mix(*waiting)
+            waiting = (r, *soften(r, scores))
+            scores = following
+        mix(*waiting)
 
     for g in range(heads_kv):
         own_copy(g).wait()
@@ -252,8 +265,9 @@
         )
 
     def finish(h, unused):
-        total = acc_buf[h, HD : HD + 1, :]
-        result = acc_buf[h, :HD, :] * (1.0 / total)
+        g, r = h // ratio, h % ratio
+        total = acc_buf[g, r, HD : HD + 1, :]
+        result = acc_buf[g, r, :HD, :] * (1.0 / total)
         out_buf[h] = result.T.astype(jnp.bfloat16)
         out_copy(h).start()
         return unused
@@ -282,22 +296,24 @@
     rows = queries.shape[0]
     heads_kv = keys_values.shape[2] // HD
     heads = band_widths.shape[0]
+    ratio = heads // heads_kv
     seq_size = lax.axis_size("seq")
-    anywhere = pl.BlockSpec(memory_space=pl.ANY)
+    outside = pl.BlockSpec(memory_space=pltpu.HBM)
     scalars = pl.BlockSpec(memory_space=pltpu.SMEM)
     dma = pltpu.SemaphoreType.DMA
     return pl.pallas_call(
-        functools.partial(attend_kernel, rows, heads_kv, heads // heads_kv),
+        functools.partial(attend_kernel, rows, heads_kv, ratio),
         out_shape=jax.ShapeDtypeStruct(queries.shape, jnp.bfloat16),
-        in_specs=[anywhere, anywhere, scalars, scalars],
-        out_specs=anywhere,
+        in_specs=[outside, outside, scalars, scalars],
+        out_specs=outside,
         scratch_shapes=[
-            pltpu.VMEM((heads, rows, HD), jnp.bfloat16),
+            pltpu.VMEM((heads_kv, ratio, rows, HD), jnp.bfloat16),
             pltpu.VMEM((seq_size, heads_kv, 2, rows, HD), jnp.bfloat16),
             pltpu.VMEM((heads_kv, HD + ONES, rows), jnp.bfloat16),
-            pltpu.VMEM((heads, HD + STAT, rows), jnp.float32),
-            pltpu.VMEM((heads, 1, rows), jnp.float32),
+            pltpu.VMEM((heads_kv, ratio, HD + STAT, rows), jnp.float32),
+            pltpu.VMEM((heads_kv, ratio, 1, rows), jnp.float32),
             pltpu.VMEM((seq_size, rows, HD), jnp.int32),
+            pltpu.VMEM((rows, rows), jnp.int32),
             pltpu.VMEM((heads, rows, HD), jnp.bfloat16),
             dma((heads,)),
             dma((heads_kv,)),

time: 30.2 us -> 19.2 us (0.64)
  Pallas kernels: 25.5 us -> 14.6 us
    pallas_call x1, Pallas kernels: 25.5 us -> 14.6 us  [fused_body(): pl.pallas_call(functools.partial(attend_kernel, rows, heads_kv, ratio), o...]
where the time goes in v1:
time: 19.2 us; the launch traced here: 19 us
  Pallas kernels  14.6 us (76%)
  local copies, waits for them, and re-layouts  4.46 us (23%)
    pallas_call x1, Pallas kernels, fused_body(): pl.pallas_call(functools.partial(attend_kernel, rows, heads_kv, ratio), o...  14.6 us
    unnamed x9, local copies, waits for them, and re-layouts  4.46 us

profile of v1, /device:TPU:31, one launch (start us, length us, event | category | flops | bytes accessed | tf_op | source)
XLA Modules:
  0.0 19.0 jit_solution(12150591825339512840)
XLA Ops:
  0.0 0.0 copy-start
  0.0 1.2 %copy-done = bf16[256,2048]{1,0:T(8,128)(2,1)S(1)} copy-done((bf16[256,2048]{1,0:T(8,128)(2,1)S(1)}, bf16[256,2048]{1,0:T(8,128)(2,1)}, u32[]{:S(2)}) %copy-start) | copy-done | bytes 1048600
  1.2 0.0 copy-start.1
  1.2 0.9 %copy-done.1 = bf16[2,256,256]{2,1,0:T(8,128)(2,1)S(1)} copy-done((bf16[2,256,256]{2,1,0:T(8,128)(2,1)S(1)}, bf16[2,256,256]{2,1,0:T(8,128)(2,1)}, u32[]{:S(2)}) %copy-start.1) | copy-done | bytes 262168
  2.2 0.0 copy-start.2
  2.2 0.7 %copy-done.2 = s32[16]{0:T(128)S(1)} copy-done((s32[16]{0:T(128)S(1)}, s32[16]{0:T(128)}, u32[]{:S(2)}) %copy-start.2) | copy-done | bytes 88
  2.8 0.0 copy-start.3
  2.8 0.7 %copy-done.3 = s32[4]{0:T(128)S(1)} copy-done((s32[4]{0:T(128)S(1)}, s32[4]{0:T(128)}, u32[]{:S(2)}) %copy-start.3) | copy-done | bytes 40
  3.5 14.6 %shard_map.46 = bf16[256,2048]{1,0:T(8,128)(2,1)S(1)} custom-call(bf16[256,2048]{1,0:T(8,128)(2,1)S(1)} %copy-done, bf16[2,256,256]{2,1,0:T(8,128)(2,1)S(1)} %copy-done.1, s32[16]{0:T(128)S(1)} %copy-done.2, s32[4]{0:T(128)S(1)} %copy-done.3), custom_call_target="tpu_custom_call" | custom-call | flops 2147483648 | bytes 2097152 | tf_op jit(solution)/shard_map/pallas_call | solution.py:304
  18.1 1.0 %copy.6 = bf16[256,2048]{1,0:T(8,128)(2,1)} copy(bf16[256,2048]{1,0:T(8,128)(2,1)S(1)} %shard_map.46) | data formatting | bytes 2097152
Async XLA Ops:
  0.0 1.2 %copy-start = (bf16[256,2048]{1,0:T(8,128)(2,1)S(1)}, bf16[256,2048]{1,0:T(8,128)(2,1)}, u32[]{:S(2)}) copy-start(bf16[256,2048]{1,0:T(8,128)(2,1)} %q_hbm.1) | copy-start | bytes 3145732
  1.2 0.9 %copy-start.1 = (bf16[2,256,256]{2,1,0:T(8,128)(2,1)S(1)}, bf16[2,256,256]{2,1,0:T(8,128)(2,1)}, u32[]{:S(2)}) copy-start(bf16[2,256,256]{2,1,0:T(8,128)(2,1)} %kv_hbm.1) | copy-start | bytes 786436
  2.2 0.7 %copy-start.2 = (s32[16]{0:T(128)S(1)}, s32[16]{0:T(128)}, u32[]{:S(2)}) copy-start(s32[16]{0:T(128)} %widths.1) | copy-start | bytes 196
  2.8 0.7 %copy-start.3 = (s32[4]{0:T(128)S(1)}, s32[4]{0:T(128)}, u32[]{:S(2)}) copy-start(s32[4]{0:T(128)} %blocks.1) | copy-start | bytes 52

commit v2 on v1

--- a/solution.py
+++ b/solution.py
@@ -156,14 +156,15 @@
     pl.semaphore_wait(barrier, seq_size - 1)
 
     for g in range(heads_kv):
+        own_copy(g).wait()
 
         @pl.when(me < 2)
         def _():
-            remote(own_rows(g), me, g, far_send.at[g], me + 2).start()
+            remote(kv_buf.at[me, g], me, g, far_send.at[g], me + 2).start()
 
         @pl.when(core == 0)
         def _():
-            remote(own_rows(g), me, g, near_send.at[g], me + 1).start()
+            remote(kv_buf.at[me, g], me, g, near_send.at[g], me + 1).start()
 
     for slot in range(seq_size):
         pos = slot * rows + lax.broadcasted_iota(jnp.int32, (rows, HD), 0)
@@ -227,8 +228,6 @@
             scores = following
         mix(*waiting)
 
-    for g in range(heads_kv):
-        own_copy(g).wait()
     for h in range(heads):
         q_copy(h).wait()
 
@@ -237,6 +236,21 @@
         return unused
 
     lax.fori_loop(0, heads_kv, own_step, 0)
+
+    def out_copy(h):
+        return pltpu.make_async_copy(
+            out_buf.at[h],
+            out_hbm.at[:, pl.ds(pl.multiple_of(h * HD, HD), HD)],
+            out_sem.at[h],
+        )
+
+    def finish(g):
+        for r in range(ratio):
+            total = acc_buf[g, r, HD : HD + 1, :]
+            result = acc_buf[g, r, :HD, :] * (1.0 / total)
+            out_buf[g * ratio + r] = result.T.astype(out_buf.dtype)
+        for r in range(ratio):
+            out_copy(g * ratio + r).start()
 
     near = heads_kv * core
 
@@ -253,36 +267,30 @@
             remote(kv_buf.at[slot, g], slot, g, pass_send.at[g], partner).start()
 
         heads_of(slot, g, False)
+
+        @pl.when((me >= 2) & (item >= near) & (lax.rem(far, 2) == 1))
+        def _():
+            finish(g)
+
         return unused
 
     lax.fori_loop(0, heads_kv * me, other_step, 0)
 
-    def out_copy(h):
-        return pltpu.make_async_copy(
-            out_buf.at[h],
-            out_hbm.at[:, pl.ds(pl.multiple_of(h * HD, HD), HD)],
-            out_sem.at[h],
-        )
-
-    def finish(h, unused):
-        g, r = h // ratio, h % ratio
-        total = acc_buf[g, r, HD : HD + 1, :]
-        result = acc_buf[g, r, :HD, :] * (1.0 / total)
-        out_buf[h] = result.T.astype(jnp.bfloat16)
-        out_copy(h).start()
+    def last_step(g, unused):
+        finish(g)
         return unused
 
-    lax.fori_loop(0, heads, finish, 0, unroll=4)
+    lax.fori_loop(0, jnp.where(me < 2, heads_kv, 0), last_step, 0)
 
     for g in range(heads_kv):
 
         @pl.when(me < 2)
         def _():
-            remote(own_rows(g), me, g, far_send.at[g], me + 2).wait_send()
+            remote(kv_buf.at[me, g], me, g, far_send.at[g], me + 2).wait_send()
 
         @pl.when(core == 0)
         def _():
-            remote(own_rows(g), me, g, near_send.at[g], me + 1).wait_send()
+            remote(kv_buf.at[me, g], me, g, near_send.at[g], me + 1).wait_send()
 
         @pl.when(me >= 2)
         def _():
@@ -326,7 +334,7 @@
         compiler_params=pltpu.CompilerParams(
             collective_id=0,
             has_side_effects=True,
-            vmem_limit_bytes=32 * 1024 * 1024,
+            vmem_limit_bytes=63 * 1024 * 1024,
         ),
         cost_estimate=pl.CostEstimate(
             flops=4 * heads * rows * rows * seq_size * HD,

time: 19.2 us -> 16.3 us (0.85)
  local copies, waits for them, and re-layouts: 4.46 us -> 2.3 us
  Pallas kernels: 14.6 us -> 13.9 us
    unnamed x9 -> x1, local copies, waits for them, and re-layouts: 4.46 us -> 2.3 us
    pallas_call x1, Pallas kernels: 14.6 us -> 13.9 us  [fused_body(): pl.pallas_call(functools.partial(attend_kernel, rows, heads_kv, ratio), o...]
where the time goes in v2:
time: 16.3 us; the launch traced here: 16.2 us
  Pallas kernels  13.9 us (85%)
  local copies, waits for them, and re-layouts  2.3 us (14%)
    pallas_call x1, Pallas kernels, fused_body(): pl.pallas_call(functools.partial(attend_kernel, rows, heads_kv, ratio), o...  13.9 us
    unnamed x1, local copies, waits for them, and re-layouts  2.3 us

profile of v2, /device:TPU:31, one launch (start us, length us, event | category | flops | bytes accessed | tf_op | source)
XLA Modules:
  0.0 16.2 jit_solution(17460129194837327547)
XLA Ops:
  0.0 13.9 %shard_map.46 = bf16[256,2048]{1,0:T(8,128)(2,1)} custom-call(bf16[256,2048]{1,0:T(8,128)(2,1)} %q_hbm.1, bf16[2,256,256]{2,1,0:T(8,128)(2,1)} %kv_hbm.1, s32[16]{0:T(128)} %widths.1, s32[4]{0:T(128)} %blocks.1), custom_call_target="tpu_custom_call" | custom-call | flops 2147483648 | bytes 2097152 | tf_op jit(solution)/shard_map/pallas_call | solution.py:312
  13.9 2.3 %copy.6 = bf16[256,2048]{1,0:T(8,128)(2,1)} copy(bf16[256,2048]{1,0:T(8,128)(2,1)} %shard_map.46) | data formatting | bytes 2097152

commit v3 on v2

--- a/solution.py
+++ b/solution.py
@@ -249,8 +249,9 @@
             total = acc_buf[g, r, HD : HD + 1, :]
             result = acc_buf[g, r, :HD, :] * (1.0 / total)
             out_buf[g * ratio + r] = result.T.astype(out_buf.dtype)
-        for r in range(ratio):
-            out_copy(g * ratio + r).start()
+            if r % 2:
+                out_copy(g * ratio + r - 1).start()
+                out_copy(g * ratio + r).start()
 
     near = heads_kv * core
 
@@ -298,6 +299,46 @@
 
     for h in range(heads):
         out_copy(h).wait()
+
+
+def move_kernel(pieces, src_hbm, dst_hbm, held, in_sem, out_sem):
+    rows = held.shape[1]
+
+    def fetch(i):
+        return pltpu.make_async_copy(
+            src_hbm.at[i * rows : (i + 1) * rows], held.at[i], in_sem.at[i]
+        )
+
+    def store(i):
+        return pltpu.make_async_copy(
+            held.at[i], dst_hbm.at[i * rows : (i + 1) * rows], out_sem.at[i]
+        )
+
+    for i in range(pieces):
+        fetch(i).start()
+    for i in range(pieces):
+        fetch(i).wait()
+        store(i).start()
+    for i in range(pieces):
+        store(i).wait()
+
+
+def move(result):
+    rows, columns = result.shape
+    pieces = 8
+    outside = pl.BlockSpec(memory_space=pltpu.HBM)
+    return pl.pallas_call(
+        functools.partial(move_kernel, pieces),
+        out_shape=jax.ShapeDtypeStruct(result.shape, result.dtype),
+        in_specs=[outside],
+        out_specs=outside,
+        scratch_shapes=[
+            pltpu.VMEM((pieces, rows // pieces, columns), result.dtype),
+            pltpu.SemaphoreType.DMA((pieces,)),
+            pltpu.SemaphoreType.DMA((pieces,)),
+        ],
+        compiler_params=pltpu.CompilerParams(vmem_limit_bytes=63 * 1024 * 1024),
+    )(result)
 
 
 def fused_body(queries, keys_values, band_widths, summary_blocks):
@@ -309,7 +350,7 @@
     outside = pl.BlockSpec(memory_space=pltpu.HBM)
     scalars = pl.BlockSpec(memory_space=pltpu.SMEM)
     dma = pltpu.SemaphoreType.DMA
-    return pl.pallas_call(
+    attended = pl.pallas_call(
         functools.partial(attend_kernel, rows, heads_kv, ratio),
         out_shape=jax.ShapeDtypeStruct(queries.shape, jnp.bfloat16),
         in_specs=[outside, outside, scalars, scalars],
@@ -342,6 +383,7 @@
             transcendentals=heads * rows * rows * seq_size,
         ),
     )(queries, keys_values, band_widths, summary_blocks)
+    return move(attended)
 
 
 def dispatch(queries, keys_values, band_widths, summary_blocks):

time: 16.3 us -> 16 us (0.982)
  local copies, waits for them, and re-layouts: 2.3 us -> 0 us
  Pallas kernels: 13.9 us -> 15.8 us
    unnamed x1 -> x0, local copies, waits for them, and re-layouts: 2.3 us -> none
    pallas_call x0 -> x1, Pallas kernels: none -> 2.09 us  [move(): pl.pallas_call(functools.partial(move_kernel, pieces), out_shape=jax.Shap...]
where the time goes in v3:
time: 16 us; the launch traced here: 15.8 us
  Pallas kernels  15.8 us (99%)
    pallas_call x1, Pallas kernels, fused_body(): pl.pallas_call(functools.partial(attend_kernel, rows, heads_kv, ratio), o...  13.7 us
    pallas_call x1, Pallas kernels, move(): pl.pallas_call(functools.partial(move_kernel, pieces), out_shape=jax.Shap...  2.09 us

profile of v3, /device:TPU:31, one launch (start us, length us, event | category | flops | bytes accessed | tf_op | source)
XLA Modules:
  0.0 15.8 jit_solution(6067937049606870488)
XLA Ops:
  0.0 13.7 %shard_map.46.src_hbm = bf16[256,2048]{1,0:T(8,128)(2,1)} custom-call(bf16[256,2048]{1,0:T(8,128)(2,1)} %q_hbm.1, bf16[2,256,256]{2,1,0:T(8,128)(2,1)} %kv_hbm.1, s32[16]{0:T(128)} %widths.1, s32[4]{0:T(128)} %blocks.1), custom_call_target="tpu_custom_call" | custom-call | flops 2147483648 | bytes 2097152 | tf_op jit(solution)/shard_map/pallas_call | solution.py:353
  13.7 2.1 %shard_map.47 = bf16[256,2048]{1,0:T(8,128)(2,1)} custom-call(bf16[256,2048]{1,0:T(8,128)(2,1)} %shard_map.46.src_hbm), custom_call_target="tpu_custom_call" | custom-call | tf_op jit(solution)/shard_map/pallas_call | solution.py:330
